TPU v7x, 32 devices: a whole 2x2x4 slice. The times are simulated.
32 devices in a mesh: dp: 8 (over y, x, core), blk: 4 (over z).
Axes of the slice: x: 2, y: 2, z: 4, core: 2. Of those that a mesh axis runs over, the one named last changes fastest.
Arguments:
- clip_embed: bfloat16 [4096, 1152], P(('dp', 'blk')), may hold values from -0.1875 to 0.1875
- caption_embed: bfloat16 [4096, 1152], P(('dp', 'blk')), may hold values from -0.1875 to 0.1875
- positive: int32 [4096], P(('dp', 'blk')), may hold values from 0 to 4095, each once
Outputs:
- clip_grad: float32 [4096, 1152], P(('dp', 'blk'))
- caption_grad: float32 [4096, 1152], P(('dp', 'blk'))
- row_loss: float32 [4096], P(('dp', 'blk'))
Inputs may be any that keep to these rules, and one draw needn't show every extreme that they name: `positive`: each caption is paired with exactly one clip.
All inputs are finite; a program needn't handle non-finite values.
Results may differ from a plain program's by a relative error of at most 0.0031.
Values may be sent and summed in bfloat16 or wider, within the bound.
A program may use at most 128 MiB of HBM per device.

v0:
```python
import jax
import jax.numpy as jnp
from jax import lax
from jax.sharding import PartitionSpec as P

TEMP = 30.0
BIAS = -8.0
EPS = 1e-06


def shifted(block, axis, distance):
    devices = range(lax.axis_size(axis))
    route = [((i - distance) % len(devices), i) for i in devices]
    return lax.ppermute(block, axis, route)


def unit_rows(embed):
    values = embed.astype(jnp.float32)
    scale = jnp.sqrt(jnp.sum(values * values, axis=1, keepdims=True) + EPS)
    return (values / scale, scale)


def pull_back(unit_f, scale, grad_unit):
    inner = jnp.sum(unit_f * grad_unit, axis=1, keepdims=True)
    return (grad_unit - unit_f * inner) / scale


def pair_tile(rows, row_pos, cols, col_ids):
    logits = TEMP * jnp.einsum("rd,cd->rc", rows, cols, preferred_element_type=jnp.float32) + BIAS
    sign = jnp.where(row_pos[:, None] == col_ids[None, :], 1.0, -1.0).astype(jnp.float32)
    loss_rows = jnp.sum(jax.nn.softplus(-sign * logits), axis=1)
    slope = (-sign * jax.nn.sigmoid(-sign * logits)).astype(jnp.bfloat16)
    grad_rows = TEMP * jnp.dot(slope, cols, preferred_element_type=jnp.float32)
    grad_cols = TEMP * jnp.einsum("rc,rd->cd", slope, rows, preferred_element_type=jnp.float32)
    return (loss_rows, grad_rows, grad_cols)


def local(clip_embed, caption_embed, positive):
    rows_dev = clip_embed.shape[0]
    width = clip_embed.shape[1]
    clip_unit, clip_scale = unit_rows(clip_embed)
    caption_unit, caption_scale = unit_rows(caption_embed)
    clip_low = clip_unit.astype(jnp.bfloat16)
    caption_low = caption_unit.astype(jnp.bfloat16)
    n_blk = lax.axis_size("blk")
    dp_index = lax.axis_index("dp")
    blk_index = lax.axis_index("blk")
    local_ids = jnp.arange(rows_dev, dtype=jnp.int32)
    group = lax.all_gather(clip_low, "dp", axis=0, tiled=True)
    group_pos = lax.all_gather(positive, "dp", axis=0, tiled=True)
    grad_sum = jnp.zeros((group.shape[0], width), jnp.float32)
    loss_sum = jnp.zeros((group.shape[0],), jnp.float32)
    held = caption_low
    travel = jnp.zeros((rows_dev, width), jnp.float32)
    for step in range(n_blk):
        anchor = dp_index * n_blk + (blk_index - step) % n_blk
        col_ids = anchor * rows_dev + local_ids
        loss_rows, grad_rows, grad_cols = pair_tile(group, group_pos, held, col_ids)
        loss_sum = loss_sum + loss_rows
        grad_sum = grad_sum + grad_rows
        travel = travel + grad_cols
        if step + 1 < n_blk:
            held = shifted(held, "blk", 1)
        travel = shifted(travel, "blk", 1)
    grad_own, loss_own = (
        lax.psum_scatter(grad_sum, "dp", scatter_dimension=0, tiled=True),
        lax.psum_scatter(loss_sum, "dp", scatter_dimension=0, tiled=True),
    )
    clip_grad = pull_back(clip_unit, clip_scale, grad_own)
    caption_grad = pull_back(caption_unit, caption_scale, travel)
    return (clip_grad, caption_grad, loss_own)


def solution(mesh):
    in_specs = (P(("dp", "blk"), None), P(("dp", "blk"), None), P(("dp", "blk")))
    out_specs = (P(("dp", "blk"), None), P(("dp", "blk"), None), P(("dp", "blk")))
    return jax.shard_map(local, mesh=mesh, in_specs=in_specs, out_specs=out_specs, check_vma=False)
```

profile of v0, /device:TPU:0, one launch (start us, length us, event | category | flops | bytes accessed | tf_op | source)
XLA Modules:
  0.0 133.8 jit_solution(17057686789014143762)
XLA Ops:
  7.2 0.0 all-gather.3.cloned.1.call-start
  7.2 1.1 fusion.10
  8.3 1.8 %fusion.16 = bf16[128,1152]{1,0:T(8,128)(2,1)} fusion(f32[128]{0:T(128)S(1)} %add_sqrt_fusion.1, bf16[128,1152]{1,0:T(8,128)(2,1)} %param.3), kind=kLoop, calls=%fused_computation.54 | loop fusion | flops 442368 | bytes 590336 | tf_op jit(solution)/shard_map/convert_element_type | solution.py:43
  10.1 0.0 all-gather.3.cloned.1.call-update
  10.2 0.0 reduce-scatter.2.cloned.1.call-start
  10.2 1.1 fusion.11
  11.3 1.1 fusion.17
  12.4 3.1 %collective-permute-start = (bf16[128,1152]{1,0:T(8,128)(2,1)S(1)}, bf16[128,1152]{1,0:T(8,128)(2,1)S(1)}, u32[]{:S(2)}, u32[]{:S(2)}) collective-permute-start(bf16[128,1152]{1,0:T(8,128)(2,1)S(1)} %fusion.17), channel_id=1, source_target_pairs={{3,0},{0,1},{1,2},{2,3},{7,4},{4,5},{5,6},{6,7},{11,8},{8,9},{9,10... | collective-permute-start | bytes 884744 | tf_op jit(solution)/shard_map/ppermute | solution.py:14
  15.5 8.8 %all-gather = s32[8,1,128]{2,1,0:T(1,128)S(1)} all-gather(s32[1,1,128]{2,1,0:T(1,128)} %bitcast.31), channel_id=1, replica_groups=mesh['dp'=8,'blk'=4] {'dp'}, dimensions={0}, use_global_device_ids=true | all-gather | bytes 4608 | tf_op jit(solution)/shard_map/all_gather | solution.py:50
  24.3 0.2 collective-permute-done
  24.5 1.4 %collective-permute-start.1 = (bf16[128,1152]{1,0:T(8,128)(2,1)S(1)}, bf16[128,1152]{1,0:T(8,128)(2,1)S(1)}, u32[]{:S(2)}, u32[]{:S(2)}) collective-permute-start(bf16[128,1152]{1,0:T(8,128)(2,1)S(1)} %collective-permute-done), channel_id=1, source_target_pairs={{3,0},{0,1},{1,2},{2,3},{7,4},{4,5},{5,6},{6,7},{11,8},{8,9},{9,10... | collective-permute-start | bytes 884744 | tf_op jit(solution)/shard_map/ppermute | solution.py:14
  25.9 9.5 %collective-permute-done.1 = bf16[128,1152]{1,0:T(8,128)(2,1)S(1)} collective-permute-done((bf16[128,1152]{1,0:T(8,128)(2,1)S(1)}, bf16[128,1152]{1,0:T(8,128)(2,1)S(1)}, u32[]{:S(2)}, u32[]{:S(2)}) %collective-permute-start.1) | collective-permute-done | bytes 294944 | tf_op jit(solution)/shard_map/ppermute | solution.py:14
  35.4 0.0 collective-permute-start.2
  35.4 6.8 %all-gather.3.cloned.1.call-done = bf16[1024,1152]{1,0:T(8,128)(2,1)} async-done(((bf16[128,1152]{1,0:T(8,128)(2,1)}), bf16[1024,1152]{1,0:T(8,128)(2,1)}) %all-gather.3.cloned.1.call-update) | async-done | bytes 2359312 | tf_op jit(solution)/shard_map/all_gather | solution.py:49
  42.2 2.8 %fusion.12 = (f32[1024]{0:T(1024)S(1)}, f32[1024,128]{0,1:T(8,128)S(1)}) fusion(bf16[1024,1152]{1,0:T(8,128)(2,1)} %all-gather.3.cloned.1.call-done, bf16[128,1152]{1,0:T(8,128)(2,1)S(1)} %fusion.17, s32[128]{0:T(128)S(1)} %iota_add_fusion.3, s32[1024]{0:T(1024)S(1)} %bitcast.19), kind=kOutput, calls=%fused_computation.35 | convolution fusion | flops 303692800 | bytes 3187200 | tf_op jit(solution)/shard_map/rd,cd->rc/dot_general | solution.py:29
  45.0 0.0 copy-start.2
  45.0 0.9 fusion.18
  45.9 0.8 copy-done.2
  46.7 1.2 fusion.14
  47.8 1.1 fusion.13
  49.0 0.0 collective-permute-done.2
  49.0 1.1 fusion.15
  50.2 0.9 convolution_add_fusion.2
  51.1 0.9 convolution_add_fusion.1
  52.0 3.0 %fusion = f32[1024,1152]{1,0:T(8,128)} fusion(f32[1024,1152]{1,0:T(8,128)S(1)} %convolution_add_fusion.1, bf16[128,1152]{1,0:T(8,128)(2,1)S(1)} %collective-permute-done.2, f32[1024,128]{0,1:T(8,128)S(1)} %get-tuple-element.4, s32[1024]{0:T(1024)S(1)} %bitcast.26, s32[128]{0:T(128)S(1)} %iota_add_fusion), kind=kOutput, calls=%fused_computation.1 | convolution fusion | flops 305397760 | bytes 10260992 | tf_op jit(solution)/shard_map/dot_general | solution.py:33
  55.0 0.0 reduce-scatter.2.cloned.1.call-update
  55.0 0.0 copy-start.3
  55.0 2.4 %convolution_multiply_fusion.3 = f32[128,1152]{1,0:T(8,128)S(1)} fusion(bf16[1024,1152]{1,0:T(8,128)(2,1)} %all-gather.3.cloned.1.call-done, f32[1024,128]{0,1:T(8,128)S(1)} %get-tuple-element.8, s32[1024]{0:T(1024)S(1)} %bitcast.27, s32[128]{0:T(128)S(1)} %iota_add_fusion.3), kind=kOutput, calls=%fused_computation.8 | convolution fusion | flops 303185920 | bytes 3478016 | tf_op jit(solution)/shard_map/rc,rd->cd/dot_general | solution.py:34
  57.4 1.5 %collective-permute-start.3 = (f32[128,1152]{1,0:T(8,128)S(1)}, f32[128,1152]{1,0:T(8,128)S(1)}, u32[]{:S(2)}, u32[]{:S(2)}) collective-permute-start(f32[128,1152]{1,0:T(8,128)S(1)} %convolution_multiply_fusion.3), channel_id=1, source_target_pairs={{3,0},{0,1},{1,2},{2,3},{7,4},{4,5},{5,6},{6,7},{11,8},{8,9},{9,10... | collective-permute-start | bytes 1769480 | tf_op jit(solution)/shard_map/ppermute | solution.py:14
  59.0 15.8 %collective-permute-done.3 = f32[128,1152]{1,0:T(8,128)S(1)} collective-permute-done((f32[128,1152]{1,0:T(8,128)S(1)}, f32[128,1152]{1,0:T(8,128)S(1)}, u32[]{:S(2)}, u32[]{:S(2)}) %collective-permute-start.3) | collective-permute-done | bytes 589856 | tf_op jit(solution)/shard_map/ppermute | solution.py:14
  74.8 0.0 copy-done.3
  74.8 0.6 fusion.1
  75.4 0.1 collective-permute-start.4
  75.5 0.6 convolution_multiply_fusion.1
  76.1 15.9 %collective-permute-done.4 = f32[128,1152]{1,0:T(8,128)S(1)} collective-permute-done((f32[128,1152]{1,0:T(8,128)S(1)}, f32[128,1152]{1,0:T(8,128)S(1)}, u32[]{:S(2)}, u32[]{:S(2)}) %collective-permute-start.4) | collective-permute-done | bytes 589856 | tf_op jit(solution)/shard_map/ppermute | solution.py:14
  91.9 0.1 add.182
  92.0 0.0 copy-start.4
  92.0 0.0 copy-start
  92.0 0.1 collective-permute-start.5
  92.1 0.6 convolution_multiply_fusion
  92.7 0.0 copy-start.1
  92.7 14.9 %collective-permute-done.5 = f32[128,1152]{1,0:T(8,128)S(1)} collective-permute-done((f32[128,1152]{1,0:T(8,128)S(1)}, f32[128,1152]{1,0:T(8,128)S(1)}, u32[]{:S(2)}, u32[]{:S(2)}) %collective-permute-start.5) | collective-permute-done | bytes 589856 | tf_op jit(solution)/shard_map/ppermute | solution.py:14
  107.6 0.1 add.183
  107.7 0.1 collective-permute-start.6
  107.8 0.0 copy-done.4
  107.8 0.6 dynamic-slice
  109.0 12.4 %all-reduce = f32[1024]{0:T(1024)S(1)} all-reduce(f32[1024]{0:T(1024)S(1)} %add_add_fusion), channel_id=3, replica_groups=mesh['dp'=8,'blk'=4] {'dp'}, use_global_device_ids=true, to_apply=%region_9.10.clone | all-reduce | flops 1024 | bytes 8192
  121.5 0.6 dynamic-slice.1
  122.0 0.3 collective-permute-done.6
  122.4 0.0 copy-done
  122.4 0.2 multiply_reduce_fusion
  122.6 1.0 subtract_divide_fusion
  123.6 0.0 reduce-scatter.2.cloned.1.call-done
  123.6 0.0 copy-done.1
  123.6 1.3 multiply_reduce_fusion.1
  124.9 2.1 %subtract_divide_fusion.1 = f32[128,1152]{1,0:T(8,128)} fusion(f32[128,1152]{1,0:T(8,128)} %reduce-scatter.2.cloned.1.call-done, f32[128]{0:T(128)S(1)} %multiply_reduce_fusion.1, f32[128]{0:T(128)S(1)} %add_sqrt_fusion.1, bf16[128,1152]{1,0:T(8,128)(2,1)S(1)} %copy-done.1), kind=kLoop, calls=%fused_computation.33 | loop fusion | flops 737280 | bytes 1475584 | tf_op jit(solution)/shard_map/div | solution.py:25
  (7 shorter events, 0.0 us)
Async XLA Ops:
  7.2 35.0 %all-gather.3.cloned.1.call-start = ((), (), s32[]{:S(2)}) async-start(), calls=%async_computation.1 | async-start | bytes 2654208 | tf_op jit(solution)/shard_map/all_gather | solution.py:49
  10.2 113.5 %reduce-scatter.2.cloned.1.call-start = ((), (), s32[]{:S(2)}) async-start(), calls=%async_computation.2 | async-start | bytes 5308416 | tf_op jit(solution)/shard_map/reduce_scatter | solution.py:66
  12.4 12.1 %collective-permute-start = (bf16[128,1152]{1,0:T(8,128)(2,1)S(1)}, bf16[128,1152]{1,0:T(8,128)(2,1)S(1)}, u32[]{:S(2)}, u32[]{:S(2)}) collective-permute-start(bf16[128,1152]{1,0:T(8,128)(2,1)S(1)} %fusion.17), channel_id=1, source_target_pairs={{3,0},{0,1},{1,2},{2,3},{7,4},{4,5},{5,6},{6,7},{11,8},{8,9},{9,10... | collective-permute-start | bytes 884744 | tf_op jit(solution)/shard_map/ppermute | solution.py:14
  24.5 10.9 %collective-permute-start.1 = (bf16[128,1152]{1,0:T(8,128)(2,1)S(1)}, bf16[128,1152]{1,0:T(8,128)(2,1)S(1)}, u32[]{:S(2)}, u32[]{:S(2)}) collective-permute-start(bf16[128,1152]{1,0:T(8,128)(2,1)S(1)} %collective-permute-done), channel_id=1, source_target_pairs={{3,0},{0,1},{1,2},{2,3},{7,4},{4,5},{5,6},{6,7},{11,8},{8,9},{9,10... | collective-permute-start | bytes 884744 | tf_op jit(solution)/shard_map/ppermute | solution.py:14
  35.4 13.6 %collective-permute-start.2 = (bf16[128,1152]{1,0:T(8,128)(2,1)S(1)}, bf16[128,1152]{1,0:T(8,128)(2,1)S(1)}, u32[]{:S(2)}, u32[]{:S(2)}) collective-permute-start(bf16[128,1152]{1,0:T(8,128)(2,1)S(1)} %collective-permute-done.1), channel_id=1, source_target_pairs={{3,0},{0,1},{1,2},{2,3},{7,4},{4,5},{5,6},{6,7},{11,8},{8,9},{9,10... | collective-permute-start | bytes 884744 | tf_op jit(solution)/shard_map/ppermute | solution.py:14
  45.0 1.7 %copy-start.2 = (bf16[1024,1152]{1,0:T(8,128)(2,1)S(1)}, bf16[1024,1152]{1,0:T(8,128)(2,1)}, u32[]{:S(2)}) copy-start(bf16[1024,1152]{1,0:T(8,128)(2,1)} %all-gather.3.cloned.1.call-done) | copy-start | bytes 7077892
  55.0 19.8 %copy-start.3 = (bf16[1024,1152]{1,0:T(8,128)(2,1)S(1)}, bf16[1024,1152]{1,0:T(8,128)(2,1)}, u32[]{:S(2)}) copy-start(bf16[1024,1152]{1,0:T(8,128)(2,1)} %all-gather.3.cloned.1.call-done) | copy-start | bytes 7077892
  57.4 17.3 %collective-permute-start.3 = (f32[128,1152]{1,0:T(8,128)S(1)}, f32[128,1152]{1,0:T(8,128)S(1)}, u32[]{:S(2)}, u32[]{:S(2)}) collective-permute-start(f32[128,1152]{1,0:T(8,128)S(1)} %convolution_multiply_fusion.3), channel_id=1, source_target_pairs={{3,0},{0,1},{1,2},{2,3},{7,4},{4,5},{5,6},{6,7},{11,8},{8,9},{9,10... | collective-permute-start | bytes 1769480 | tf_op jit(solution)/shard_map/ppermute | solution.py:14
  75.4 16.5 %collective-permute-start.4 = (f32[128,1152]{1,0:T(8,128)S(1)}, f32[128,1152]{1,0:T(8,128)S(1)}, u32[]{:S(2)}, u32[]{:S(2)}) collective-permute-start(f32[128,1152]{1,0:T(8,128)S(1)} %fusion.1), channel_id=1, source_target_pairs={{3,0},{0,1},{1,2},{2,3},{7,4},{4,5},{5,6},{6,7},{11,8},{8,9},{9,10... | collective-permute-start | bytes 1769480 | tf_op jit(solution)/shard_map/ppermute | solution.py:14
  92.0 15.8 %copy-start.4 = (u32[32]{0:T(128)S(1)}, u32[32]{0:T(128)}, u32[]{:S(2)}) copy-start(u32[32]{0:T(128)} %constant.67) | copy-start | bytes 388
  92.0 30.4 %copy-start = (bf16[128,1152]{1,0:T(8,128)(2,1)S(1)}, bf16[128,1152]{1,0:T(8,128)(2,1)}, u32[]{:S(2)}) copy-start(bf16[128,1152]{1,0:T(8,128)(2,1)} %param.4) | copy-start | bytes 884740
  92.0 15.6 %collective-permute-start.5 = (f32[128,1152]{1,0:T(8,128)S(1)}, f32[128,1152]{1,0:T(8,128)S(1)}, u32[]{:S(2)}, u32[]{:S(2)}) collective-permute-start(f32[128,1152]{1,0:T(8,128)S(1)} %add.182), channel_id=1, source_target_pairs={{3,0},{0,1},{1,2},{2,3},{7,4},{4,5},{5,6},{6,7},{11,8},{8,9},{9,10... | collective-permute-start | bytes 1769480 | tf_op jit(solution)/shard_map/ppermute | solution.py:14
  92.7 30.9 %copy-start.1 = (bf16[128,1152]{1,0:T(8,128)(2,1)S(1)}, bf16[128,1152]{1,0:T(8,128)(2,1)}, u32[]{:S(2)}) copy-start(bf16[128,1152]{1,0:T(8,128)(2,1)} %param.3) | copy-start | bytes 884740
  107.7 14.7 %collective-permute-start.6 = (f32[128,1152]{1,0:T(8,128)S(1)}, f32[128,1152]{1,0:T(8,128)S(1)}, u32[]{:S(2)}, u32[]{:S(2)}) collective-permute-start(f32[128,1152]{1,0:T(8,128)S(1)} %add.183), channel_id=1, source_target_pairs={{3,0},{0,1},{1,2},{2,3},{7,4},{4,5},{5,6},{6,7},{11,8},{8,9},{9,10... | collective-permute-start | bytes 1769480 | tf_op jit(solution)/shard_map/ppermute | solution.py:14
Sparse Core Ops, SparseCore 0:
  10.5 31.7 all-gather.2
  55.1 53.9 reduce-scatter.1
where the time goes:
time: 134 us
  waiting for transfers between devices  63.4 us (47%)
  blocking collectives  21.3 us (16%)
  matrix products  16.2 us (12%)
  between operations  14.9 us (11%)
  other arithmetic  9.88 us (7%)
  starting transfers between devices  6.28 us (5%)
  local copies, waits for them, and re-layouts  1.96 us (1%)
    ppermute x7, waiting for transfers between devices, shifted(): return lax.ppermute(block, axis, route)  56.6 us
    unnamed x1, blocking collectives  12.4 us
    all_gather x1, blocking collectives, local(): group_pos = lax.all_gather(positive, 'dp', axis=0, tiled=True)  8.85 us
    all_gather x1, waiting for transfers between devices, local(): group = lax.all_gather(clip_low, 'dp', axis=0, tiled=True)  6.77 us
    dot_general x4, matrix products, pair_tile(): jnp.einsum('rd,cd->rc', rows, cols, preferred_element_type=jnp.float32)  6.25 us
    ppermute x7, starting transfers between devices, shifted(): return lax.ppermute(block, axis, route)  6.21 us
    dot_general x4, matrix products, pair_tile(): grad_rows = TEMP * jnp.dot(slope, cols, preferred_element_type=jnp.float32)  5.71 us
    dot_general x4, matrix products, pair_tile(): jnp.einsum('rc,rd->cd', slope, rows, preferred_element_type=jnp.float32)  4.22 us
  transfers between devices with their start and end apart: 9, of which 7 were waited for; matrix products, arithmetic and copies ran while one was open for 11% of the time, Pallas kernels for 0%

commit v1 on v0

v1 whole, which is shorter than its diff:
```python
import functools

import jax
import jax.numpy as jnp
from jax import lax
from jax.experimental import pallas as pl
from jax.experimental.pallas import tpu as pltpu
from jax.sharding import PartitionSpec as P

TEMP = 30.0
BIAS = -8.0
EPS = 1e-06
MESH = pl.DeviceIdType.MESH
BF = jnp.bfloat16
F32 = jnp.float32


def unit_rows(embed):
    values = embed.astype(F32)
    scale = jnp.sqrt(jnp.sum(values * values, axis=1, keepdims=True) + EPS)
    return values / scale, scale


def pull_back(embed, grad_unit):
    unit_f, scale = unit_rows(embed)
    inner = jnp.sum(unit_f * grad_unit, axis=1, keepdims=True)
    return (grad_unit - unit_f * inner) / scale


def kernel(Y, X, NZ, clip_ref, cap_ref, pos_ref, clip_out, cap_out, loss_out,
           clips, caps, capown, pos, pt, loss, capacc, xsend, xrecv, zsend, zrecv,
           csend, crecv, lcrecv, yacc, ysend, yrecv, lyrecv, zcsend, zcrecv, lzrecv,
           ssem, clip_r, pos_r, cap_r, x_r, z_r, c_r, y_r, zc_r, l_r):
    R, D = clip_ref.shape
    dp = lax.axis_index("dp")
    z = lax.axis_index("blk")
    c = dp % 2
    x = (dp // 2) % X
    y = dp // (2 * X)
    sib = 1 - c
    zr = z % 2
    zo = 1 - zr
    zc = z + 1 - 2 * zr

    def dev(yy, xx, cc, zz):
        return ((yy * X + xx) * 2 + cc, zz)

    def rows(slot, n=1):
        return pl.ds(pl.multiple_of(slot * R, R), n * R)

    def slot_of(cc, yy, k):
        return (cc * Y + yy) * 2 + k

    count = [0]
    sent = []

    def send(src, dst, rsem, where, cond=None):
        copy = pltpu.make_async_remote_copy(
            src_ref=src, dst_ref=dst, send_sem=ssem.at[count[0]], recv_sem=rsem,
            device_id=where, device_id_type=MESH)
        count[0] += 1
        sent.append((copy, cond))
        if cond is None:
            copy.start()
        else:
            pl.when(cond)(copy.start)

    def arrive(dst, rsem):
        pltpu.make_async_remote_copy(
            src_ref=dst, dst_ref=dst, send_sem=ssem.at[0], recv_sem=rsem,
            device_id=dev(y, x, sib, z), device_id_type=MESH).wait_recv()

    ys = [(y + d) % Y for d in range(1, Y)]
    xs = [(x + d) % X for d in range(1, X)]
    peers = [dev(y, x, c, (z + d) % NZ) for d in range(1, NZ)]
    peers += [dev(yy, x, c, z) for yy in ys] + [dev(y, xx, c, z) for xx in xs]
    peers += [dev(y, x, sib, z)]
    barrier = pltpu.get_barrier_semaphore()
    for peer in peers:
        pl.semaphore_signal(barrier, inc=1, device_id=peer, device_id_type=MESH)

    mine = slot_of(c, y, zr)
    other = slot_of(c, y, zo)
    clips[rows(mine), :] = unit_rows(clip_ref[...])[0].astype(BF)
    capown[...] = unit_rows(cap_ref[...])[0].astype(BF)
    pos[c, y, zr] = pos_ref[0]
    pl.semaphore_wait(barrier, len(peers))

    send(clips.at[rows(mine)], clips.at[rows(mine)], clip_r.at[mine], dev(y, x, c, zc))
    send(pos.at[c, y, zr], pos.at[c, y, zr], pos_r.at[0], dev(y, x, c, zc))
    for j in range(2):
        to = z // 2 + 2 * j
        slot = zr * X + x
        send(capown, caps.at[rows(slot)], cap_r.at[slot], dev(y, x, c, to), to != z)
    for yy in ys:
        send(clips.at[rows(mine)], clips.at[rows(mine)], clip_r.at[mine], dev(yy, x, c, z))
    send(clips.at[rows(mine)], clips.at[rows(mine)], clip_r.at[mine], dev(y, x, sib, z))
    for k in range(2):
        w = 2 * zr + k
        slot = k * X + x

        @pl.when(w == z)
        def _():
            caps[rows(slot), :] = capown[...]

        for xx in xs:
            send(caps.at[rows(slot)], caps.at[rows(slot)], cap_r.at[slot], dev(y, xx, c, z), w == z)
    arrive(clips.at[rows(other)], clip_r.at[other])
    for yy in ys:
        send(clips.at[rows(other)], clips.at[rows(other)], clip_r.at[other], dev(yy, x, c, z))
    send(clips.at[rows(other)], clips.at[rows(other)], clip_r.at[other], dev(y, x, sib, z))
    arrive(pos.at[c, y, zo], pos_r.at[0])
    for yy in ys:
        send(pos.at[c, y], pos.at[c, y], pos_r.at[1 + y], dev(yy, x, c, z))
    for k in range(2):
        w = 2 * zr + k
        slot = k * X + x

        @pl.when(w != z)
        def _():
            arrive(caps.at[rows(slot)], cap_r.at[slot])

        for xx in xs:
            send(caps.at[rows(slot)], caps.at[rows(slot)], cap_r.at[slot], dev(y, xx, c, z), w != z)
    for k in (zr, zo):
        for yy in ys:
            slot = slot_of(c, yy, k)
            arrive(clips.at[rows(slot)], clip_r.at[slot])
            send(clips.at[rows(slot)], clips.at[rows(slot)], clip_r.at[slot], dev(y, x, sib, z))
    for yy in ys:
        arrive(pos.at[c, yy], pos_r.at[1 + yy])
    send(pos.at[c], pos.at[c], pos_r.at[1 + Y], dev(y, x, sib, z))
    for k in range(2):
        for xx in xs:
            slot = k * X + xx
            arrive(caps.at[rows(slot)], cap_r.at[slot])
    for yy in range(Y):
        for k in range(2):
            slot = slot_of(sib, yy, k)
            arrive(clips.at[rows(slot)], clip_r.at[slot])
    arrive(pos.at[sib], pos_r.at[1 + Y])

    half = X * R
    tile = lax.broadcasted_iota(jnp.int32, (half, 1), 0)
    cap_dev = (y * X + tile // R) * 2 + c

    def scores(i, _):
        k = i // (2 * Y)
        b = i % (2 * Y)
        cc = b // Y
        yy = b % Y
        cols = pl.ds(pl.multiple_of(b * 2 * R, 2 * R), 2 * R)
        sel = pl.ds(pl.multiple_of(k * half, half), half)
        dots = lax.dot_general(caps[sel, :], clips[cols, :], (((1,), (1,)), ((), ())),
                               preferred_element_type=F32)
        logits = TEMP * dots + BIAS
        ids = (cap_dev * NZ + 2 * zr + k) * R + tile % R
        both = pos[cc, yy]
        target = jnp.concatenate([both[0], both[1]], axis=1)
        hit = ids == target
        t = jnp.where(hit, -logits, logits)
        a = jnp.exp(-jnp.abs(t))
        soft = jnp.maximum(t, 0.0) + jnp.log1p(a)
        sig = jnp.where(t >= 0.0, 1.0, a) / (1.0 + a)
        pt[sel, cols] = jnp.where(hit, -sig, sig).astype(BF)
        part = jnp.sum(soft, axis=0, keepdims=True)
        for m in range(2):
            old = jnp.where(k == 0, 0.0, loss[cc, yy, m])
            loss[cc, yy, m] = old + part[:, m * R:(m + 1) * R]
        return 0

    loss[...] = jnp.zeros_like(loss)
    lax.fori_loop(0, 4 * Y, scores, 0)
    send(loss.at[sib], lcrecv, l_r.at[0], dev(y, x, sib, z))

    def clip_part(cc, yy):
        cols = pl.ds(pl.multiple_of((cc * Y + yy) * 2 * R, 2 * R), 2 * R)
        return TEMP * lax.dot_general(pt[:, cols], caps[...], (((0,), (0,)), ((), ())),
                                      preferred_element_type=F32)

    for yy in ys + [y]:
        csend[yy] = clip_part(sib, yy).astype(BF)
        send(csend.at[yy], crecv.at[yy], c_r.at[yy], dev(y, x, sib, z))

    for k in range(2):
        for xx in xs + [x]:
            slot = k * X + xx
            g = TEMP * jnp.dot(pt[rows(slot), :], clips[...], preferred_element_type=F32)
            if xx is x:
                capacc[k] = g
            else:
                xsend[slot] = g.astype(BF)
                send(xsend.at[slot], xrecv.at[k * X + x], x_r.at[k * X + x], dev(y, xx, c, z))

    arrive(lcrecv, l_r.at[0])
    loss[c] = loss[c] + lcrecv[...]
    for yy in ys:
        send(loss.at[c, yy], lyrecv.at[y], l_r.at[1 + y], dev(yy, x, c, z))
    for yy in ys:
        g = clip_part(c, yy)
        arrive(crecv.at[yy], c_r.at[yy])
        ysend[yy] = (g + crecv[yy].astype(F32)).astype(BF)
        for k in (zo, zr):
            send(ysend.at[yy, rows(k)], yrecv.at[y, rows(k)], y_r.at[y, k], dev(yy, x, c, z))
    g = clip_part(c, y)
    arrive(crecv.at[y], c_r.at[y])
    yacc[...] = g + crecv[y].astype(F32)

    for k in range(2):
        w = 2 * zr + k
        for xx in xs:
            arrive(xrecv.at[k * X + xx], x_r.at[k * X + xx])
            capacc[k] = capacc[k] + xrecv[k * X + xx].astype(F32)
        zsend[k] = capacc[k].astype(BF)
        send(zsend.at[k], zrecv.at[z // 2], z_r.at[z // 2], dev(y, x, c, w), w != z)

    for yy in ys:
        arrive(lyrecv.at[yy], l_r.at[1 + yy])
        loss[c, y] = loss[c, y] + lyrecv[yy]
    send(loss.at[c, y, zo], lzrecv, l_r.at[1 + Y], dev(y, x, c, zc))
    for yy in ys:
        arrive(yrecv.at[yy, rows(zo)], y_r.at[yy, zo])
        yacc[rows(zo), :] = yacc[rows(zo), :] + yrecv[yy, rows(zo), :].astype(F32)
    zcsend[...] = yacc[rows(zo), :].astype(BF)
    send(zcsend, zcrecv, zc_r.at[0], dev(y, x, c, zc))
    for yy in ys:
        arrive(yrecv.at[yy, rows(zr)], y_r.at[yy, zr])
        yacc[rows(zr), :] = yacc[rows(zr), :] + yrecv[yy, rows(zr), :].astype(F32)

    arrive(lzrecv, l_r.at[1 + Y])
    loss_out[...] = loss[c, y, zr] + lzrecv[...]
    cap_out[...] = jnp.zeros_like(cap_out)
    for j in range(2):
        p = z // 2 + 2 * j

        @pl.when(p == z)
        def _():
            cap_out[...] = cap_out[...] + capacc[z % 2]

        @pl.when(p != z)
        def _():
            arrive(zrecv.at[j], z_r.at[j])
            cap_out[...] = cap_out[...] + zrecv[j].astype(F32)

    cap_out[...] = pull_back(cap_ref[...], cap_out[...])
    arrive(zcrecv, zc_r.at[0])
    clip_out[...] = pull_back(clip_ref[...], yacc[rows(zr), :] + zcrecv[...].astype(F32))

    for copy, cond in sent:
        if cond is None:
            copy.wait_send()
        else:
            pl.when(cond)(copy.wait_send)


def local(Y, X, NZ, clip_embed, caption_embed, positive):
    R, D = clip_embed.shape
    ncl, ncap = 4 * Y, 2 * X
    V = pltpu.VMEM
    dma = pltpu.SemaphoreType.DMA
    scratch = [
        V((ncl * R, D), BF), V((ncap * R, D), BF), V((R, D), BF),
        V((2, Y, 2, 1, R), jnp.int32), V((ncap * R, ncl * R), BF), V((2, Y, 2, 1, R), F32),
        V((2, R, D), F32), V((ncap, R, D), BF), V((ncap, R, D), BF), V((2, R, D), BF), V((2, R, D), BF),
        V((Y, 2 * R, D), BF), V((Y, 2 * R, D), BF), V((Y, 2, 1, R), F32),
        V((2 * R, D), F32), V((Y, 2 * R, D), BF), V((Y, 2 * R, D), BF), V((Y, 2, 1, R), F32),
        V((R, D), BF), V((R, D), BF), V((1, R), F32),
        dma((16 + 12 * (X + Y),)), dma((ncl,)), dma((2 + Y,)), dma((ncap,)), dma((ncap,)), dma((2,)),
        dma((Y,)), dma((Y, 2)), dma((1,)), dma((2 + Y,)),
    ]
    vm = pl.BlockSpec(memory_space=V)
    clip_grad, cap_grad, loss = pl.pallas_call(
        functools.partial(kernel, Y, X, NZ),
        out_shape=(jax.ShapeDtypeStruct((R, D), F32), jax.ShapeDtypeStruct((R, D), F32),
                   jax.ShapeDtypeStruct((1, R), F32)),
        in_specs=[vm] * 3, out_specs=(vm,) * 3, scratch_shapes=scratch,
        compiler_params=pltpu.CompilerParams(
            collective_id=0, has_side_effects=True, vmem_limit_bytes=56 * 1024 * 1024),
    )(clip_embed, caption_embed, positive.reshape(1, 1, R))
    return clip_grad, cap_grad, loss.reshape(R)


def solution(mesh):
    n_dp, n_blk = mesh.shape["dp"], mesh.shape["blk"]
    assert n_blk == 4 and n_dp % 2 == 0
    plane = n_dp // 2
    Y = max(d for d in range(1, plane + 1) if plane % d == 0 and d * d <= plane)
    X = plane // Y
    specs = (P(("dp", "blk"), None), P(("dp", "blk"), None), P(("dp", "blk")))
    return jax.shard_map(functools.partial(local, Y, X, n_blk), mesh=mesh, in_specs=specs,
                         out_specs=specs, check_vma=False)
```

time: 134 us -> 66.2 us (0.49)
  waiting for transfers between devices: 63.4 us -> 0 us
  Pallas kernels: 0 us -> 61.2 us
  blocking collectives: 21.3 us -> 0 us
  matrix products: 16.2 us -> 0 us
  between operations: 14.9 us -> 0.65 us
  other arithmetic: 9.88 us -> 0 us
  starting transfers between devices: 6.28 us -> 0 us
  local copies, waits for them, and re-layouts: 1.96 us -> 3.31 us
    pallas_call x0 -> x1, Pallas kernels: none -> 61.2 us  [local(): pl.pallas_call(functools.partial(kernel, Y, X, NZ), out_shape=(jax.ShapeD...]
    ppermute x7 -> x0, waiting for transfers between devices: 56.6 us -> none  [shifted(): return lax.ppermute(block, axis, route)]
    dot_general x12 -> x0, matrix products: 16.2 us -> none  [the longest x4 6.25 us: pair_tile(): jnp.einsum('rd,cd->rc', rows, cols, preferred_element_type=jnp.float32)]
    unnamed x1 -> x0, blocking collectives: 12.4 us -> none
    all_gather x1 -> x0, blocking collectives: 8.85 us -> none  [local(): group_pos = lax.all_gather(positive, 'dp', axis=0, tiled=True)]
    all_gather x1 -> x0, waiting for transfers between devices: 6.77 us -> none  [local(): group = lax.all_gather(clip_low, 'dp', axis=0, tiled=True)]
    ppermute x7 -> x0, starting transfers between devices: 6.21 us -> none  [shifted(): return lax.ppermute(block, axis, route)]
    reduce_sum x4 -> x0, other arithmetic: 3.74 us -> none  [the longest x2 2.21 us: unit_rows(): scale = jnp.sqrt(jnp.sum(values * values, axis=1, keepdims=True) + EPS)]
  transfers between devices with their start and end apart: 9 -> 0, of which waited for: 7 -> 0; matrix products, arithmetic and copies ran while one was open for 11% -> 0% of each run, Pallas kernels for 0% -> 0%
where the time goes in v1:
time: 66.2 us; the launch traced here: 65.2 us
  Pallas kernels  61.2 us (92%)
  local copies, waits for them, and re-layouts  3.31 us (5%)
    pallas_call x1, Pallas kernels, local(): pl.pallas_call(functools.partial(kernel, Y, X, NZ), out_shape=(jax.ShapeD...  61.2 us
    unnamed x7, local copies, waits for them, and re-layouts  3.31 us

profile of v1, /device:TPU:0, one launch (start us, length us, event | category | flops | bytes accessed | tf_op | source)
XLA Modules:
  0.0 65.2 jit_solution(16562792396561878258)
XLA Ops:
  0.6 61.2 %shard_map.58 = (f32[128,1152]{1,0:T(8,128)}, f32[128,1152]{1,0:T(8,128)}, f32[1,128]{1,0:T(1,128)}) custom-call(bf16[128,1152]{1,0:T(8,128)(2,1)} %clip_ref.1, bf16[128,1152]{1,0:T(8,128)(2,1)} %cap_ref.1, s32[1,1,128]{2,1,0:T(1,128)} %bitcast.2), custom_call_target="tpu_custom_call" | custom-call | tf_op jit(solution)/shard_map/pallas_call | solution.py:272
  61.9 0.0 copy-start
  61.9 2.0 %copy.9 = f32[128,1152]{1,0:T(8,128)} copy(f32[128,1152]{1,0:T(8,128)} %get-tuple-element.12) | data formatting | bytes 1179648
  63.9 0.0 copy-done
  63.9 0.0 copy-start.1
  63.9 0.8 %copy.10 = f32[128,1152]{1,0:T(8,128)} copy(f32[128,1152]{1,0:T(8,128)S(1)} %copy-done) | data formatting | bytes 1179648
  64.7 0.0 copy-done.1
  64.7 0.5 copy.11
Async XLA Ops:
  61.9 2.0 %copy-start = (f32[128,1152]{1,0:T(8,128)S(1)}, f32[128,1152]{1,0:T(8,128)}, u32[]{:S(2)}) copy-start(f32[128,1152]{1,0:T(8,128)} %get-tuple-element.13) | copy-start | bytes 1769476
  63.9 0.8 %copy-start.1 = (f32[1,128]{1,0:T(1,128)S(1)}, f32[1,128]{1,0:T(1,128)}, u32[]{:S(2)}) copy-start(f32[1,128]{1,0:T(1,128)} %get-tuple-element.8) | copy-start | bytes 1540

commit v2 on v1

v2 whole, which is shorter than its diff:
```python
import functools

import jax
import jax.numpy as jnp
from jax import lax
from jax.experimental import pallas as pl
from jax.experimental.pallas import tpu as pltpu
from jax.sharding import PartitionSpec as P

TEMP = 30.0
BIAS = -8.0
EPS = 1e-06
MESH = pl.DeviceIdType.MESH
BF = jnp.bfloat16
F32 = jnp.float32
NG = 4
NP = 2
WS = 2


def unit_rows(embed):
    values = embed.astype(F32)
    scale = jnp.sqrt(jnp.sum(values * values, axis=1, keepdims=True) + EPS)
    return values / scale, scale


def pull_back(embed, grad_unit):
    unit_f, scale = unit_rows(embed)
    inner = jnp.sum(unit_f * grad_unit, axis=1, keepdims=True)
    return (grad_unit - unit_f * inner) / scale


def kernel(Y, X, NZ, clip_ref, cap_ref, pos_ref, clip_out, cap_out, loss_out,
           clips, caps, capown, pos, pt, loss, capacc, xsend, xrecv, zsend, zrecv,
           csend, crecv, lcrecv, acc, yacc, ysend, yrecv, lyrecv, zcsend, zcrecv, lzrecv,
           ssem, clip_r, pos_r, cap_r, x_r, z_r, c_r, y_r, zc_r, l_r):
    R, D = clip_ref.shape
    H, HG = R // NP, R // NG
    dp = lax.axis_index("dp")
    z = lax.axis_index("blk")
    c = dp % 2
    x = (dp // 2) % X
    y = dp // (2 * X)
    sib = 1 - c
    zr = z % 2
    zo = 1 - zr
    zc = z + 1 - 2 * zr

    def dev(yy, xx, cc, zz):
        return ((yy * X + xx) * 2 + cc, zz)

    def rows(slot, n=1):
        return pl.ds(pl.multiple_of(slot * R, R), n * R)

    def piece(slot, p):
        return pl.ds(pl.multiple_of(slot * R + p * HG, HG), HG)

    def slot_of(cc, yy, k):
        return (k * Y + yy) * 2 + cc

    count = [0]
    sent = []

    def send(src, dst, rsem, where, cond=None):
        copy = pltpu.make_async_remote_copy(
            src_ref=src, dst_ref=dst, send_sem=ssem.at[count[0]], recv_sem=rsem,
            device_id=where, device_id_type=MESH)
        count[0] += 1
        sent.append((copy, cond))
        if cond is None:
            copy.start()
        else:
            pl.when(cond)(copy.start)

    done = set()

    def settle(first, last=None):
        for i in range(first, len(sent) if last is None else last):
            if i in done:
                continue
            done.add(i)
            copy, cond = sent[i]
            if cond is None:
                copy.wait_send()
            else:
                pl.when(cond)(copy.wait_send)

    def arrive(dst, rsem):
        pltpu.make_async_remote_copy(
            src_ref=dst, dst_ref=dst, send_sem=ssem.at[0], recv_sem=rsem,
            device_id=dev(y, x, sib, z), device_id_type=MESH).wait_recv()

    ys = [(y + d) % Y for d in range(1, Y)]
    xs = [(x + d) % X for d in range(1, X)]
    peers = [dev(y, x, c, (z + d) % NZ) for d in range(1, NZ)]
    peers += [dev(yy, x, c, z) for yy in ys] + [dev(y, xx, c, z) for xx in xs]
    peers += [dev(y, x, sib, z)]
    barrier = pltpu.get_barrier_semaphore()
    for peer in peers:
        pl.semaphore_signal(barrier, inc=1, device_id=peer, device_id_type=MESH)

    mine = slot_of(c, y, zr)
    other = slot_of(c, y, zo)
    clips[rows(mine), :] = unit_rows(clip_ref[...])[0].astype(BF)
    capown[...] = unit_rows(cap_ref[...])[0].astype(BF)
    pos[c, y, zr] = pos_ref[0]
    pl.semaphore_wait(barrier, len(peers))

    owner = 3 * zr == z
    passer = jnp.logical_not(owner)
    for p in range(NG):
        part = clips.at[piece(mine, p)]
        send(part, part, clip_r.at[mine, p], dev(y, x, c, zc))
        for j in range(2):
            to = z // 2 + 2 * j
            slot = zr * X + x
            send(capown.at[pl.ds(p * HG, HG)], caps.at[piece(slot, p)], cap_r.at[slot, p],
                 dev(y, x, c, to), to != z)
    send(pos.at[c, y, zr], pos.at[c, y, zr], pos_r.at[0], dev(y, x, c, zc))
    whole = clips.at[rows(mine)]
    for yy in ys:
        send(whole, whole, clip_r.at[mine, 0], dev(yy, x, c, z))
    send(whole, whole, clip_r.at[mine, 0], dev(y, x, sib, z))
    near, far = zr * X + x, zo * X + x

    @pl.when(owner)
    def _():
        caps[rows(near), :] = capown[...]

    for p in range(NG):
        part = caps.at[piece(near, p)]
        for xx in xs:
            send(part, part, cap_r.at[near, p], dev(y, xx, c, z), owner)
    for p in range(NG):
        part = clips.at[piece(other, p)]
        arrive(part, clip_r.at[other, p])
        for yy in ys:
            send(part, part, clip_r.at[other, p], dev(yy, x, c, z))
        part = caps.at[piece(far, p)]
        arrive(part, cap_r.at[far, p])
        for xx in xs:
            send(part, part, cap_r.at[far, p], dev(y, xx, c, z))
        part = caps.at[piece(near, p)]

        @pl.when(passer)
        def _():
            arrive(part, cap_r.at[near, p])

        for xx in xs:
            send(part, part, cap_r.at[near, p], dev(y, xx, c, z), passer)
    whole = clips.at[rows(other)]
    send(whole, whole, clip_r.at[other, 0], dev(y, x, sib, z))
    arrive(pos.at[c, y, zo], pos_r.at[0])
    for yy in ys:
        send(pos.at[c, y], pos.at[c, y], pos_r.at[1 + y], dev(yy, x, c, z))
    for yy in ys:
        slot = slot_of(c, yy, zr)
        whole = clips.at[rows(slot)]
        arrive(whole, clip_r.at[slot, 0])
        send(whole, whole, clip_r.at[slot, 0], dev(y, x, sib, z))
    for yy in ys:
        arrive(pos.at[c, yy], pos_r.at[1 + yy])
    send(pos.at[c], pos.at[c], pos_r.at[1 + Y], dev(y, x, sib, z))
    for yy in ys:
        slot = slot_of(c, yy, zo)
        for p in range(NG):
            arrive(clips.at[piece(slot, p)], clip_r.at[slot, p])
        whole = clips.at[rows(slot)]
        send(whole, whole, clip_r.at[slot, 0], dev(y, x, sib, z))
    for k in range(2):
        for xx in xs:
            slot = k * X + xx
            for p in range(NG):
                arrive(caps.at[piece(slot, p)], cap_r.at[slot, p])
    for yy in range(Y):
        for k in range(2):
            slot = slot_of(sib, yy, k)
            arrive(clips.at[rows(slot)], clip_r.at[slot, 0])
    arrive(pos.at[sib], pos_r.at[1 + Y])

    half = X * R
    tile = lax.broadcasted_iota(jnp.int32, (half, 1), 0)
    cap_dev = (y * X + tile // R) * 2 + c

    def scores(k, kk, yy):
        b = kk * Y + yy
        cols = pl.ds(pl.multiple_of(b * 2 * R, 2 * R), 2 * R)
        sel = pl.ds(pl.multiple_of(k * half, half), half)
        dots = lax.dot_general(caps[sel, :], clips[cols, :], (((1,), (1,)), ((), ())),
                               preferred_element_type=F32)
        logits = TEMP * dots + BIAS
        ids = (cap_dev * NZ + 2 * zr + k) * R + tile % R
        target = jnp.concatenate([pos[0, yy, kk], pos[1, yy, kk]], axis=1)
        hit = ids == target
        t = jnp.where(hit, -logits, logits)
        a = jnp.exp(-jnp.abs(t))
        soft = jnp.maximum(t, 0.0) + jnp.log1p(a)
        sig = jnp.where(t >= 0.0, 1.0, a) / (1.0 + a)
        pt[sel, cols] = jnp.where(hit, -sig, sig).astype(BF)
        part = jnp.sum(soft, axis=0, keepdims=True)
        for m in range(2):
            loss[m, yy, kk] = loss[m, yy, kk] + part[:, m * R:(m + 1) * R]

    loss[...] = jnp.zeros_like(loss)

    def cap_part(k, xx):
        return TEMP * jnp.dot(pt[rows(k * X + xx), :], clips[...], preferred_element_type=F32)

    def clip_part(k, yy):
        both = pl.ds(pl.multiple_of((k * Y + yy) * 2 * R, 2 * R), 2 * R)
        acc[...] = TEMP * lax.dot_general(pt[:, both], caps[...], (((0,), (0,)), ((), ())),
                                          preferred_element_type=F32)
        csend[k, yy] = acc[rows(sib), :].astype(BF)
        send(csend.at[k, yy], crecv.at[k, yy], c_r.at[k, yy], dev(y, x, sib, z))
        yacc[k, yy] = acc[rows(c), :]

    def clip_both(k, yy):
        arrive(crecv.at[k, yy], c_r.at[k, yy])
        return yacc[k, yy] + crecv[k, yy].astype(F32)

    def cap_on(k, p, cond):
        part = pl.ds(p * H, H)
        g = capacc[k, part]
        for xx in xs:
            arrive(xrecv.at[k * X + xx, part], x_r.at[k * X + xx, p])
            g = g + xrecv[k * X + xx, part].astype(F32)
        capacc[k, part] = g
        zsend[k, part] = g.astype(BF)
        send(zsend.at[k, part], zrecv.at[z // 2, part], z_r.at[z // 2, p], dev(y, x, c, 2 * zr + k), cond)

    def clip_own(k, p):
        part = pl.ds(p * H, H)
        g = yacc[k, y, part]
        for yy in ys:
            arrive(yrecv.at[k, yy, part], y_r.at[k, yy, p])
            g = g + yrecv[k, yy, part].astype(F32)
        return g

    def cap_ready(k):
        for xx in xs:
            xsend[k * X + xx] = cap_part(k, xx).astype(BF)

    def clip_ready(k):
        for yy in ys:
            ysend[k, yy] = clip_both(k, yy).astype(BF)

    def issue_x(s):
        k, part = (zo if s < NP else zr), pl.ds(s % NP * H, H)
        for xx in xs:
            send(xsend.at[k * X + xx, part], xrecv.at[k * X + x, part], x_r.at[k * X + x, s % NP], dev(y, xx, c, z))

    def issue_y(s):
        k, part = (zo if s < NP else zr), pl.ds(s % NP * H, H)
        for yy in ys:
            send(ysend.at[k, yy, part], yrecv.at[k, y, part], y_r.at[k, y, s % NP], dev(yy, x, c, z))

    def issue(s):
        if s >= WS:
            settle(*waves[s - WS])
        first = len(sent)
        issue_x(s)
        issue_y(s)
        waves.append((first, len(sent)))

    def landed(s):
        p = s % NP
        part = pl.ds(p * H, H)
        if s < NP:
            cap_on(zo, p, None)
            zcsend[part] = clip_own(zo, p).astype(BF)
            send(zcsend.at[part], zcrecv.at[part], zc_r.at[p], dev(y, x, c, zc))
        else:
            cap_on(zr, p, passer)
            yacc[zr, y, part] = clip_own(zr, p)

    for yy in ys:
        scores(zo, zo, yy)
        scores(zr, zo, yy)
        clip_part(zo, yy)
    scores(zo, zo, y)
    for yy in range(Y):
        scores(zo, zr, yy)
    cap_ready(zo)
    waves = []
    clip_ready(zo)
    issue(0)
    scores(zr, zo, y)
    for yy in range(Y):
        scores(zr, zr, yy)
    issue(1)
    send(loss.at[sib], lcrecv, l_r.at[0], dev(y, x, sib, z))
    capacc[zo] = cap_part(zo, x)
    clip_part(zo, y)
    if NP > 2:
        issue(2)
    for yy in ys:
        clip_part(zr, yy)
    yacc[zo, y] = clip_both(zo, y)
    if NP > 2:
        landed(0)
        issue(3)
    cap_ready(zr)
    if NP > 2:
        landed(1)
    clip_ready(zr)
    issue(NP)
    arrive(lcrecv, l_r.at[0])
    loss[c] = loss[c] + lcrecv[...]
    for yy in ys:
        send(loss.at[c, yy], lyrecv.at[y], l_r.at[1 + y], dev(yy, x, c, z))
    clip_part(zr, y)
    landed(NP - 2)
    issue(NP + 1)
    capacc[zr] = cap_part(zr, x)
    landed(NP - 1)
    if NP > 2:
        issue(6)
    yacc[zr, y] = clip_both(zr, y)
    landed(NP)
    if NP > 2:
        issue(7)
        landed(5)
    for yy in ys:
        arrive(lyrecv.at[yy], l_r.at[1 + yy])
        loss[c, y] = loss[c, y] + lyrecv[yy]
    send(loss.at[c, y, zo], lzrecv, l_r.at[1 + Y], dev(y, x, c, zc))
    for s in range(2 * NP - 2 if NP > 2 else 3, 2 * NP):
        landed(s)

    for p in range(NP):
        arrive(zcrecv.at[pl.ds(p * H, H)], zc_r.at[p])
    clip_out[...] = yacc[zr, y] + zcrecv[...].astype(F32)
    arrive(lzrecv, l_r.at[1 + Y])
    loss_out[...] = loss[c, y, zr] + lzrecv[...]
    for j in range(2):
        plane = z // 2 + 2 * j

        @pl.when(plane == z)
        def _():
            cap_out[j] = capacc[zr]

        @pl.when(plane != z)
        def _():
            for p in range(NP):
                arrive(zrecv.at[j, pl.ds(p * H, H)], z_r.at[j, p])
            cap_out[j] = zrecv[j].astype(F32)

    settle(0)


def finish(clip_ref, cap_ref, clip_sum, cap_sum, loss_sum, clip_out, cap_out, loss_out):
    clip_out[...] = pull_back(clip_ref[...], clip_sum[...])
    cap_out[...] = pull_back(cap_ref[...], cap_sum[0] + cap_sum[1])
    loss_out[...] = loss_sum[...]


def local(Y, X, NZ, clip_embed, caption_embed, positive):
    R, D = clip_embed.shape
    ncl, ncap = 4 * Y, 2 * X
    V = pltpu.VMEM
    dma = pltpu.SemaphoreType.DMA
    scratch = [
        V((ncl * R, D), BF), V((ncap * R, D), BF), V((R, D), BF),
        V((2, Y, 2, 1, R), jnp.int32), V((ncap * R, ncl * R), BF), V((2, Y, 2, 1, R), F32),
        V((2, R, D), F32), V((ncap, R, D), BF), V((ncap, R, D), BF), V((2, R, D), BF), V((2, R, D), BF),
        V((2, Y, R, D), BF), V((2, Y, R, D), BF), V((Y, 2, 1, R), F32),
        V((2 * R, D), F32), V((2, Y, R, D), F32), V((2, Y, R, D), BF), V((2, Y, R, D), BF), V((Y, 2, 1, R), F32),
        V((R, D), BF), V((R, D), BF), V((1, R), F32),
        dma((32 + 32 * (X + Y),)), dma((ncl, NG)), dma((2 + Y,)), dma((ncap, NG)), dma((ncap, NP)), dma((2, NP)),
        dma((2, Y)), dma((2, Y, NP)), dma((NP,)), dma((2 + Y,)),
    ]
    vm = pl.BlockSpec(memory_space=V)
    sums = pl.pallas_call(
        functools.partial(kernel, Y, X, NZ),
        out_shape=(jax.ShapeDtypeStruct((R, D), F32), jax.ShapeDtypeStruct((2, R, D), F32),
                   jax.ShapeDtypeStruct((1, R), F32)),
        in_specs=[vm] * 3, out_specs=(vm,) * 3, scratch_shapes=scratch,
        compiler_params=pltpu.CompilerParams(
            collective_id=0, has_side_effects=True, vmem_limit_bytes=56 * 1024 * 1024),
    )(clip_embed, caption_embed, positive.reshape(1, 1, R))
    clip_grad, cap_grad, loss = pl.pallas_call(
        finish,
        out_shape=(jax.ShapeDtypeStruct((R, D), F32), jax.ShapeDtypeStruct((R, D), F32),
                   jax.ShapeDtypeStruct((1, R), F32)),
        in_specs=[vm] * 5, out_specs=(vm,) * 3,
    )(clip_embed, caption_embed, *sums)
    return clip_grad, cap_grad, loss.reshape(R)


def solution(mesh):
    n_dp, n_blk = mesh.shape["dp"], mesh.shape["blk"]
    assert n_blk == 4 and n_dp % 2 == 0
    plane = n_dp // 2
    Y = max(d for d in range(1, plane + 1) if plane % d == 0 and d * d <= plane)
    X = plane // Y
    specs = (P(("dp", "blk"), None), P(("dp", "blk"), None), P(("dp", "blk")))
    return jax.shard_map(functools.partial(local, Y, X, n_blk), mesh=mesh, in_specs=specs,
                         out_specs=specs, check_vma=False)
```

time: 66.2 us -> 57 us (0.86); the launches traced: 65.2 us -> 56.8 us
  Pallas kernels: 61.2 us -> 56.2 us
  local copies, waits for them, and re-layouts: 3.31 us -> 0 us
    pallas_call x1, Pallas kernels: 61.2 us -> 53.2 us  [local(): pl.pallas_call(functools.partial(kernel, Y, X, NZ), out_shape=(jax.ShapeD...]
    unnamed x7 -> x0, local copies, waits for them, and re-layouts: 3.31 us -> none
    pallas_call x0 -> x1, Pallas kernels: none -> 3 us  [local(): pl.pallas_call(finish, out_shape=(jax.ShapeDtypeStruct((R, D), F32), jax....]
where the time goes in v2:
time: 57 us; the launch traced here: 56.8 us
  Pallas kernels  56.2 us (99%)
  between operations  0.64 us (1%)
    pallas_call x1, Pallas kernels, local(): pl.pallas_call(functools.partial(kernel, Y, X, NZ), out_shape=(jax.ShapeD...  53.2 us
    pallas_call x1, Pallas kernels, local(): pl.pallas_call(finish, out_shape=(jax.ShapeDtypeStruct((R, D), F32), jax....  3 us

profile of v2, /device:TPU:0, one launch (start us, length us, event | category | flops | bytes accessed | tf_op | source)
XLA Modules:
  0.0 56.8 jit_solution(11555616067986270151)
XLA Ops:
  0.6 53.2 %shard_map.58 = (f32[128,1152]{1,0:T(8,128)}, f32[2,128,1152]{2,1,0:T(8,128)}, f32[1,128]{1,0:T(1,128)}) custom-call(bf16[128,1152]{1,0:T(8,128)(2,1)} %clip_ref.3, bf16[128,1152]{1,0:T(8,128)(2,1)} %cap_ref.3, s32[1,1,128]{2,1,0:T(1,128)} %bitcast.2), custom_call_target="tpu_custom_call" | custom-call | tf_op jit(solution)/shard_map/pallas_call | solution.py:373
  53.8 3.0 %shard_map.59 = (f32[128,1152]{1,0:T(8,128)}, f32[128,1152]{1,0:T(8,128)}, f32[1,128]{1,0:T(1,128)}) custom-call(bf16[128,1152]{1,0:T(8,128)(2,1)} %clip_ref.3, bf16[128,1152]{1,0:T(8,128)(2,1)} %cap_ref.3, f32[128,1152]{1,0:T(8,128)} %get-tuple-element.9.clip_sum, f32[2,128,1152]{2,1,0:T(8,128)} %get-tuple-element.10.cap_sum, ...), custom_call_target="tpu_custom_call" | custom-call | tf_op jit(solution)/shard_map/pallas_call | solution.py:381

commit v3 on v2

--- a/solution.py
+++ b/solution.py
@@ -14,8 +14,9 @@
 BF = jnp.bfloat16
 F32 = jnp.float32
 NG = 4
-NP = 2
-WS = 2
+NP = 4
+WS = 3
+WZ = 9
 
 
 def unit_rows(embed):
@@ -108,7 +109,12 @@
 
     owner = 3 * zr == z
     passer = jnp.logical_not(owner)
-    for p in range(NG):
+    zmarks = []
+
+    def gather_z(p):
+        if p >= WZ:
+            settle(*zmarks[p - WZ])
+        begin = len(sent)
         part = clips.at[piece(mine, p)]
         send(part, part, clip_r.at[mine, p], dev(y, x, c, zc))
         for j in range(2):
@@ -116,6 +122,10 @@
             slot = zr * X + x
             send(capown.at[pl.ds(p * HG, HG)], caps.at[piece(slot, p)], cap_r.at[slot, p],
                  dev(y, x, c, to), to != z)
+        zmarks.append((begin, len(sent)))
+
+    for p in range(min(WZ, NG)):
+        gather_z(p)
     send(pos.at[c, y, zr], pos.at[c, y, zr], pos_r.at[0], dev(y, x, c, zc))
     whole = clips.at[rows(mine)]
     for yy in ys:
@@ -131,6 +141,8 @@
         part = caps.at[piece(near, p)]
         for xx in xs:
             send(part, part, cap_r.at[near, p], dev(y, xx, c, z), owner)
+    for p in range(WZ, NG):
+        gather_z(p)
     for p in range(NG):
         part = clips.at[piece(other, p)]
         arrive(part, clip_r.at[other, p])
@@ -337,20 +349,20 @@
 
         @pl.when(plane == z)
         def _():
-            cap_out[j] = capacc[zr]
+            cap_out[...] = capacc[zr] if j == 0 else cap_out[...] + capacc[zr]
 
         @pl.when(plane != z)
         def _():
             for p in range(NP):
                 arrive(zrecv.at[j, pl.ds(p * H, H)], z_r.at[j, p])
-            cap_out[j] = zrecv[j].astype(F32)
+            cap_out[...] = zrecv[j].astype(F32) if j == 0 else cap_out[...] + zrecv[j].astype(F32)
 
     settle(0)
 
 
 def finish(clip_ref, cap_ref, clip_sum, cap_sum, loss_sum, clip_out, cap_out, loss_out):
     clip_out[...] = pull_back(clip_ref[...], clip_sum[...])
-    cap_out[...] = pull_back(cap_ref[...], cap_sum[0] + cap_sum[1])
+    cap_out[...] = pull_back(cap_ref[...], cap_sum[...])
     loss_out[...] = loss_sum[...]
 
 
@@ -372,7 +384,7 @@
     vm = pl.BlockSpec(memory_space=V)
     sums = pl.pallas_call(
         functools.partial(kernel, Y, X, NZ),
-        out_shape=(jax.ShapeDtypeStruct((R, D), F32), jax.ShapeDtypeStruct((2, R, D), F32),
+        out_shape=(jax.ShapeDtypeStruct((R, D), F32), jax.ShapeDtypeStruct((R, D), F32),
                    jax.ShapeDtypeStruct((1, R), F32)),
         in_specs=[vm] * 3, out_specs=(vm,) * 3, scratch_shapes=scratch,
         compiler_params=pltpu.CompilerParams(

time: 57 us -> 55.1 us (0.967)
  Pallas kernels: 56.2 us -> 54.3 us
    pallas_call x1, Pallas kernels: 53.2 us -> 51.5 us  [local(): pl.pallas_call(functools.partial(kernel, Y, X, NZ), out_shape=(jax.ShapeD...]
where the time goes in v3:
time: 55.1 us; the launch traced here: 54.9 us
  Pallas kernels  54.3 us (99%)
  between operations  0.64 us (1%)
    pallas_call x1, Pallas kernels, local(): pl.pallas_call(functools.partial(kernel, Y, X, NZ), out_shape=(jax.ShapeD...  51.5 us
    pallas_call x1, Pallas kernels, local(): pl.pallas_call(finish, out_shape=(jax.ShapeDtypeStruct((R, D), F32), jax....  2.8 us

profile of v3, /device:TPU:0, one launch (start us, length us, event | category | flops | bytes accessed | tf_op | source)
XLA Modules:
  0.0 54.9 jit_solution(2660714949050919174)
XLA Ops:
  0.6 51.5 %shard_map.58 = (f32[128,1152]{1,0:T(8,128)}, f32[128,1152]{1,0:T(8,128)}, f32[1,128]{1,0:T(1,128)}) custom-call(bf16[128,1152]{1,0:T(8,128)(2,1)} %clip_ref.3, bf16[128,1152]{1,0:T(8,128)(2,1)} %cap_ref.3, s32[1,1,128]{2,1,0:T(1,128)} %bitcast.2), custom_call_target="tpu_custom_call" | custom-call | tf_op jit(solution)/shard_map/pallas_call | solution.py:385
  52.1 2.8 %shard_map.59 = (f32[128,1152]{1,0:T(8,128)}, f32[128,1152]{1,0:T(8,128)}, f32[1,128]{1,0:T(1,128)}) custom-call(bf16[128,1152]{1,0:T(8,128)(2,1)} %clip_ref.3, bf16[128,1152]{1,0:T(8,128)(2,1)} %cap_ref.3, f32[128,1152]{1,0:T(8,128)} %get-tuple-element.9.clip_sum, f32[128,1152]{1,0:T(8,128)} %get-tuple-element.10.cap_sum, f32[1,128]{1,0:T(1,128)} %get-tuple-element.11.loss_sum), custom_call_target="tpu_custom_call" | custom-call | tf_op jit(solution)/shard_map/pallas_call | solution.py:393
